TPU v7x, 128 devices: a whole 4x4x4 slice. The times are simulated.
128 devices in a mesh: row: 16 (over y, x_lo, core), col: 8 (over z, x_hi).
Axes of the slice: x: 4 (x_hi: 2, x_lo: 2; x = x_hi * 2 + x_lo), y: 4, z: 4, core: 2. Of those that a mesh axis runs over, the one named last changes fastest.
Arguments:
- grad_flat: bfloat16 [8192, 4096], P(('row', 'col')), may hold values from -6 to 6
- out_factor_inv: bfloat16 [8192, 8192], P('row', 'col'), may hold values from -0.05 to 2.05
- in_factor_inv: bfloat16 [4096, 16384], P(('row', 'col')), may hold values from -0.05 to 2.05
Outputs:
- preconditioned: float32 [8192, 16384], P('row', 'col')
All inputs are finite; a program needn't handle non-finite values.
Results may differ from a plain program's by a relative error of at most 0.003.
Values may be sent and summed in bfloat16 or wider, within the bound.
A program may use at most 128 MiB of HBM per device.

v0:
```python
import jax
import jax.numpy as jnp
from jax import lax
from jax.sharding import PartitionSpec as P


def per_device(grad_flat, out_factor_inv, in_factor_inv):
    grad_block, factor_block = (
        lax.all_to_all(grad_flat, "col", split_axis=1, concat_axis=0, tiled=True),
        lax.all_to_all(in_factor_inv, "col", split_axis=1, concat_axis=0, tiled=True),
    )
    grad_panel = lax.all_gather(grad_block, "row", axis=0, tiled=True)
    factor_rows = lax.all_gather(out_factor_inv, "col", axis=1, tiled=True)
    product = jnp.dot(factor_rows, grad_panel, preferred_element_type=jnp.float32)
    product_wide = lax.all_gather(product.astype(jnp.bfloat16), "col", axis=1, tiled=True)
    gathered = lax.all_gather(factor_block, "row", axis=0, tiled=True)
    result = jnp.dot(product_wide, gathered, preferred_element_type=jnp.float32)
    return result


def solution(mesh):
    return jax.shard_map(
        per_device,
        mesh=mesh,
        in_specs=(P(("row", "col"), None), P("row", "col"), P(("row", "col"), None)),
        out_specs=P("row", "col"),
        check_vma=False,
    )
```

profile of v0, /device:TPU:1, one launch (start us, length us, event | category | flops | bytes accessed | tf_op | source)
XLA Modules:
  0.0 376.2 jit_solution(13584681474714637482)
XLA Ops:
  6.5 0.0 all-gather.5.cloned.1.call-start
  6.5 0.7 all-gather.5.cloned.1.call-update
  7.3 0.0 all-gather.7.cloned.1.call-start
  7.3 1.1 copy.13
  8.4 18.9 %all_to_all.38 = bf16[64,8,512]{2,0,1:T(8,128)(2,1)} all-to-all(bf16[64,8,512]{2,0,1:T(8,128)(2,1)S(1)} %bitcast.21), channel_id=1, replica_groups=mesh['row'=16,'col'=8] {'col'}, dimensions={1} | all-to-all | bytes 1048576 | tf_op jit(solution)/shard_map/all_to_all | solution.py:9
  27.3 0.0 all-gather.7.cloned.1.call-update
  27.3 0.0 copy-start
  27.3 0.0 all-gather.9.cloned.1.call-start
  27.4 92.4 %all-gather.5.cloned.1.call-done = bf16[512,8192]{1,0:T(8,128)(2,1)} async-done(((bf16[512,1024]{1,0:T(8,128)(2,1)}), bf16[512,8192]{1,0:T(8,128)(2,1)}) %all-gather.5.cloned.1.call-update) | async-done | bytes 8388624 | tf_op jit(solution)/shard_map/all_gather | solution.py:13
  119.8 52.4 %all-gather.7.cloned.1.call-done = bf16[8192,512]{1,0:T(8,128)(2,1)} async-done(((bf16[512,512]{1,0:T(8,128)(2,1)}), bf16[8192,512]{1,0:T(8,128)(2,1)}) %all-gather.7.cloned.1.call-update) | async-done | bytes 8388624 | tf_op jit(solution)/shard_map/all_gather | solution.py:12
  172.2 11.0 %convolution_convert_fusion = bf16[512,512]{1,0:T(8,128)(2,1)} fusion(bf16[512,8192]{1,0:T(8,128)(2,1)} %all-gather.5.cloned.1.call-done, bf16[8192,512]{1,0:T(8,128)(2,1)} %all-gather.7.cloned.1.call-done), kind=kOutput, calls=%fused_computation | convolution fusion | flops 4295229440 | bytes 17301504 | tf_op jit(solution)/shard_map/dot_general | solution.py:14
  183.2 0.0 all-gather.9.cloned.1.call-update
  183.3 0.0 all-gather.11.cloned.1.call-start
  183.3 0.0 copy-done
  183.3 0.1 copy.12
  183.4 28.6 %all_to_all.39 = bf16[32,8,2048]{2,0,1:T(8,128)(2,1)} all-to-all(bf16[32,8,2048]{2,0,1:T(8,128)(2,1)S(1)} %bitcast.19), channel_id=1, replica_groups=mesh['row'=16,'col'=8] {'col'}, dimensions={1} | all-to-all | bytes 2097152 | tf_op jit(solution)/shard_map/all_to_all | solution.py:10
  212.0 0.0 all-gather.11.cloned.1.call-update
  212.0 50.9 %all-gather.9.cloned.1.call-done = bf16[512,4096]{1,0:T(8,128)(2,1)} async-done(((bf16[512,512]{1,0:T(8,128)(2,1)}), bf16[512,4096]{1,0:T(8,128)(2,1)}) %all-gather.9.cloned.1.call-update) | async-done | bytes 4194320 | tf_op jit(solution)/shard_map/all_gather | solution.py:15
  263.0 91.8 %all-gather.11.cloned.1.call-done = bf16[4096,2048]{1,0:T(8,128)(2,1)} async-done(((bf16[256,2048]{1,0:T(8,128)(2,1)}), bf16[4096,2048]{1,0:T(8,128)(2,1)}) %all-gather.11.cloned.1.call-update) | async-done | bytes 16777232 | tf_op jit(solution)/shard_map/all_gather | solution.py:16
  354.8 14.9 %fusion = f32[512,2048]{1,0:T(8,128)} fusion(bf16[512,4096]{1,0:T(8,128)(2,1)} %all-gather.9.cloned.1.call-done, bf16[4096,2048]{1,0:T(8,128)(2,1)} %all-gather.11.cloned.1.call-done), kind=kOutput, calls=%fused_computation.3 | convolution fusion | flops 8589934592 | bytes 25165824 | tf_op jit(solution)/shard_map/dot_general | solution.py:17
Async XLA Ops:
  6.5 113.2 %all-gather.5.cloned.1.call-start = ((), (), s32[]{:S(2)}) async-start(), calls=%async_computation.2 | async-start | bytes 9437184 | tf_op jit(solution)/shard_map/all_gather | solution.py:13
  7.3 164.9 %all-gather.7.cloned.1.call-start = ((), (), s32[]{:S(2)}) async-start(), calls=%async_computation.3 | async-start | bytes 8912896 | tf_op jit(solution)/shard_map/all_gather | solution.py:12
  27.3 156.0 %copy-start = (bf16[32,16384]{1,0:T(8,128)(2,1)S(1)}, bf16[32,16384]{1,0:T(8,128)(2,1)}, u32[]{:S(2)}) copy-start(bf16[32,16384]{1,0:T(8,128)(2,1)} %param.5) | copy-start | bytes 3145732
  27.3 235.6 %all-gather.9.cloned.1.call-start = ((), (), s32[]{:S(2)}) async-start(), calls=%async_computation.4 | async-start | bytes 4718592 | tf_op jit(solution)/shard_map/all_gather | solution.py:15
  183.3 171.5 %all-gather.11.cloned.1.call-start = ((), (), s32[]{:S(2)}) async-start(), calls=%async_computation.5 | async-start | bytes 17825792 | tf_op jit(solution)/shard_map/all_gather | solution.py:16
Sparse Core Ops, SparseCore 0:
  9.7 110.0 all-gather.4
  121.5 50.6 all-gather.6
  183.4 79.5 all-gather.8
  264.5 90.2 all-gather.10
where the time goes:
time: 376 us
  waiting for transfers between devices  288 us (77%)
  blocking collectives  47.5 us (13%)
  matrix products  25.9 us (7%)
  between operations  13.2 us (4%)
    all_gather x1, waiting for transfers between devices, per_device(): factor_rows = lax.all_gather(out_factor_inv, 'col', axis=1, tiled=True)  92.4 us
    all_gather x1, waiting for transfers between devices, per_device(): gathered = lax.all_gather(factor_block, 'row', axis=0, tiled=True)  91.8 us
    all_gather x1, waiting for transfers between devices, per_device(): grad_panel = lax.all_gather(grad_block, 'row', axis=0, tiled=True)  52.4 us
    all_gather x1, waiting for transfers between devices, per_device(): lax.all_gather(product.astype(jnp.bfloat16), 'col', axis=1, tiled=True)  50.9 us
    all_to_all x1, blocking collectives, per_device(): lax.all_to_all(in_factor_inv, 'col', split_axis=1, concat_axis=0, tiled=T...  28.6 us
    all_to_all x1, blocking collectives, per_device(): lax.all_to_all(grad_flat, 'col', split_axis=1, concat_axis=0, tiled=True)  18.9 us
    dot_general x1, matrix products, per_device(): result = jnp.dot(product_wide, gathered, preferred_element_type=jnp.float32)  14.9 us
    dot_general x1, matrix products, per_device(): jnp.dot(factor_rows, grad_panel, preferred_element_type=jnp.float32)  11 us
  transfers between devices with their start and end apart: 4, of which 4 were waited for; matrix products, arithmetic and copies ran while one was open for 0% of the time, Pallas kernels for 0%

commit v1 on v0

v1 whole, which is shorter than its diff:
```python
import functools

import jax
import jax.numpy as jnp
from jax import lax
from jax.experimental import pallas as pl
from jax.experimental.pallas import tpu as pltpu
from jax.sharding import PartitionSpec as P

MESH = pl.DeviceIdType.MESH

PARTS = {"A": 2, "L": 2, "G": 2, "F": 4}
UNITS = {"A": 1.0, "L": 0.5, "G": 0.5, "F": 0.5}
RELIEF = {"A": True, "L": True, "G": False, "F": False}
OWN = -1


def plan(array, slot, part):
    ahead, behind = ("+", "-") if part % 2 == 0 else ("-", "+")
    sends = {
        OWN: [("x", 0), (ahead, 1), (behind, 2)],
        0: [(ahead, 3)] + ([] if RELIEF[array] else [(behind, 4)]),
        1: [(ahead, 5)],
        2: [("x", 4)] if RELIEF[array] else [],
        4: [(behind, 6)],
    }.get(slot, [])
    if array in "GF" and slot < 7:
        sends = sends + [("core", 8 + slot)]
    return sends


def relative(slot, part):
    sibling, slot = (1, slot - 8) if slot >= 7 else (0, slot)
    step, other = {OWN: (0, 0), 0: (0, 1), 1: (3, 0), 2: (1, 0), 3: (3, 1), 4: (1, 1), 5: (2, 0), 6: (2, 1)}[slot]
    return (step if part % 2 == 0 else (4 - step) % 4), other, sibling


def schedule():
    free, pending, order = {}, [], []
    unit = 11.3

    def send(now, array, slot, part):
        for link, there in plan(array, slot, part):
            key = link if link in ("x", "core") else link + ("z" if array in "AL" else "y")
            took = UNITS[array] * (unit if link != "core" else 1.8)
            start = max(now, free.get(key, 0.0))
            free[key] = start + took
            pending.append((start + took + 1.0, array, there, part))

    for key in ("x", "+z", "-z"):
        free[key] = 17.0
    pending += [(1.0, "A", OWN, p) for p in range(PARTS["A"])]
    pending += [(8.0, "G", OWN, p) for p in range(PARTS["G"])]
    pending += [(24.0, "F", OWN, p) for p in range(PARTS["F"])]
    seen = {}
    while pending:
        pending.sort()
        event = pending.pop(0)
        now, array, slot, part = event
        order.append(event)
        send(now, array, slot, part)
        seen.setdefault((array, part), []).append(now)
        if array == "G" and sum(len(seen.get(("G", p), [])) for p in range(PARTS["G"])) == 16 * PARTS["G"]:
            seen["G"] = now
        if array in "AG" and "G" in seen:
            for p in range(PARTS["A"]):
                if len(seen.get(("A", p), [])) == 8 and ("L", p) not in seen:
                    seen[("L", p)] = []
                    pending.append((now + 1.5, "L", OWN, p))
    return order


def pick(index, values):
    chosen = values[0]
    for position, value in enumerate(values[1:], 1):
        chosen = jnp.where(index == position, value, chosen)
    return chosen


def kernel(order, grad, outer, inner, result, a_buf, g_buf, f_buf, l_buf, l_sum, c_sum, *sems):
    send_sem = dict(zip("AGFL", sems[0:4]))
    recv_sem = dict(zip("AGFL", sems[4:8]))
    swap_send, swap_recv, local_sem, out_sem = sems[8:]
    row, col = lax.axis_index("row"), lax.axis_index("col")
    y, x_lo, core = row // 4, (row // 2) % 2, row % 2
    z, x_hi = col // 2, col % 2

    def row_of(step, other, sibling=0):
        return ((y + step) % 4) * 4 + (x_lo + other) % 2 * 2 + (core + sibling) % 2

    def col_of(step, other):
        return ((z + step) % 4) * 2 + (x_hi + other) % 2

    def device(array, link):
        if link == "core":
            return (row_of(0, 0, 1), col)
        step, other = {"x": (0, 1), "+": (1, 0), "-": (3, 0)}[link]
        return (row, col_of(step, other)) if array in "AL" else (row_of(step, other), col)

    def block_id(array, slot, part):
        step, other, sibling = relative(slot, part)
        return col_of(step, other) if array in "AL" else row_of(step, other, sibling)

    buffers = {"A": a_buf, "G": g_buf, "F": f_buf, "L": l_buf}

    def view(array, block, part):
        buffer = buffers[array]
        if array == "F":
            width = buffer.shape[2] // PARTS["F"]
            return buffer.at[block, :, pl.ds(part * width, width)]
        height = buffer.shape[1] // PARTS[array]
        return buffer.at[block, pl.ds(part * height, height), :]

    def copy(array, slot, part, link, there):
        here = view(array, block_id(array, slot, part), part)
        return pltpu.make_async_remote_copy(
            src_ref=here,
            dst_ref=here,
            send_sem=send_sem[array].at[there, part],
            recv_sem=recv_sem[array].at[there, part],
            device_id=device(array, link),
            device_id_type=MESH,
        )

    def wait_recv(array, slot, part):
        here = view(array, block_id(array, slot, part), part)
        pltpu.make_async_remote_copy(
            src_ref=here,
            dst_ref=here,
            send_sem=send_sem[array].at[slot, part],
            recv_sem=recv_sem[array].at[slot, part],
            device_id=device(array, "x"),
            device_id_type=MESH,
        ).wait_recv()

    sent = []

    def forward(array, slot, part):
        for link, there in plan(array, slot, part):
            outgoing = copy(array, slot, part, link, there)
            outgoing.start()
            sent.append(outgoing)

    locals_ = [
        pltpu.make_async_copy(outer, a_buf.at[col], local_sem.at[0]),
        pltpu.make_async_copy(
            grad.at[:, pl.ds(pl.multiple_of(col * 512, 512), 512)],
            g_buf.at[row, pl.ds(pl.multiple_of(col * 64, 64), 64), :],
            local_sem.at[1],
        ),
        pltpu.make_async_copy(
            inner.at[:, pl.ds(pl.multiple_of(col * 2048, 2048), 2048)],
            f_buf.at[row, pl.ds(pl.multiple_of(col * 32, 32), 32), :],
            local_sem.at[2],
        ),
    ]
    for one in locals_:
        one.start()

    barrier = pltpu.get_barrier_semaphore()
    peers = [(row, lax.rem(col + k, 8)) for k in range(1, 8)]
    peers += [device("G", link) for link in ("x", "+", "-", "core")]
    for peer in peers:
        pl.semaphore_signal(barrier, inc=1, device_id=peer, device_id_type=MESH)
    pl.semaphore_wait(barrier, len(peers))

    def swap(which, k):
        source, buffer, height, width = ((grad, g_buf, 64, 512), (inner, f_buf, 32, 2048))[which]
        to = lax.rem(col + k, 8)
        return pltpu.make_async_remote_copy(
            src_ref=source.at[:, pl.ds(pl.multiple_of(to * width, width), width)],
            dst_ref=buffer.at[row, pl.ds(pl.multiple_of(col * height, height), height), :],
            send_sem=swap_send.at[which, k],
            recv_sem=swap_recv.at[which, k],
            device_id=(row, to),
            device_id_type=MESH,
        )

    def swap_wait(which, k):
        source, buffer, height, width = ((grad, g_buf, 64, 512), (inner, f_buf, 32, 2048))[which]
        sender = lax.rem(col + 8 - k, 8)
        pltpu.make_async_remote_copy(
            src_ref=source.at[:, pl.ds(0, width)],
            dst_ref=buffer.at[row, pl.ds(pl.multiple_of(sender * height, height), height), :],
            send_sem=swap_send.at[which, k],
            recv_sem=swap_recv.at[which, k],
            device_id=(row, sender),
            device_id_type=MESH,
        ).wait_recv()

    def start_swap(which):
        for k in (4, 3, 5, 2, 6, 1, 7):
            outgoing = swap(which, k)
            outgoing.start()
            sent.append(outgoing)

    start_swap(0)

    def add_left(block, part):
        rows = pl.ds(part * 256 if isinstance(part, int) else pl.multiple_of(part * 256, 256), 256)
        grads = g_buf[pl.ds(block * 2, 2)].reshape(1024, 512)
        l_sum[rows, :] += jnp.dot(a_buf[block, rows, :], grads, preferred_element_type=jnp.float32)

    def add_result(block, part):
        columns = pl.ds(part * 512 if isinstance(part, int) else pl.multiple_of(part * 512, 512), 512)
        weights = f_buf[pl.ds(block * 2, 2), :, columns].reshape(512, 512)
        c_sum[:, columns] += jnp.dot(l_buf[block], weights, preferred_element_type=jnp.float32)

    def each(pairs, act):
        if len(pairs) < 2:
            for pair in pairs:
                act(*pair)
            return

        @pl.loop(0, len(pairs))
        def _(k):
            act(pick(k, [p[0] for p in pairs]), pick(k, [p[1] for p in pairs]))

    counts = dict.fromkeys("AGFL", 0)
    counts.update({("F", p): 0 for p in range(PARTS["F"])})
    pending_left, ready_l, ready_f, out_copies = [], [], [], []
    blocks_l = {}
    done = [0] * PARTS["F"]

    def multiply(pairs):
        last = any(done[p] == 7 for _, p in pairs)
        for group in [[pair] for pair in pairs] if last else [pairs]:
            each(group, add_result)
            for _, p in group:
                done[p] += 1
                if done[p] == 8:
                    columns = pl.ds(p * 512, 512)
                    out = pltpu.make_async_copy(c_sum.at[:, columns], result.at[:, columns], out_sem.at[p])
                    out.start()
                    out_copies.append(out)

    for _, array, slot, part in order:
        if slot == OWN:
            if array == "A":
                if part == 0:
                    locals_[0].wait()
                forward("A", OWN, part)
                if part == PARTS["A"] - 1:
                    start_swap(1)
                    l_sum[...] = jnp.zeros_like(l_sum)

                    @pl.loop(0, 8)
                    def _(k):
                        rows = pl.ds(pl.multiple_of(k * 64, 64), 64)
                        c_sum[rows, :] = jnp.zeros((64, 2048), jnp.float32)
            elif array == "L":
                l_buf[col, pl.ds(part * 256, 256), :] = l_sum[pl.ds(part * 256, 256), :].astype(jnp.bfloat16)
                forward("L", OWN, part)
            else:
                which = "GF".index(array)
                if part == 0:
                    locals_[1 + which].wait()
                    for k in range(1, 8):
                        swap_wait(which, k)
                forward(array, OWN, part)
        else:
            wait_recv(array, slot, part)
            if slot < 7:
                forward(array, slot, part)
        counts[array] += 1
        if array == "A":
            pending_left.append((block_id("A", slot, part), part))
        if array in "AG" and counts["G"] == 16 * PARTS["G"]:
            each(pending_left, add_left)
            pending_left.clear()
        if array == "L":
            place = relative(slot, part)
            blocks_l[place] = blocks_l.get(place, 0) + 1
            if blocks_l[place] == PARTS["L"]:
                ready_l.append(block_id("L", slot, part))
                multiply([(ready_l[-1], p) for p in ready_f])
        if array == "F":
            counts[("F", part)] += 1
            if counts[("F", part)] == 16:
                ready_f.append(part)
                multiply([(block, part) for block in ready_l])

    for one in sent:
        one.wait_send()
    for out in out_copies:
        out.wait()


def per_device(grad_flat, out_factor_inv, in_factor_inv):
    order = schedule()
    dma = pltpu.SemaphoreType.DMA
    return pl.pallas_call(
        functools.partial(kernel, order),
        out_shape=jax.ShapeDtypeStruct((512, 2048), jnp.float32),
        in_specs=[pl.BlockSpec(memory_space=pl.ANY)] * 3,
        out_specs=pl.BlockSpec(memory_space=pl.ANY),
        scratch_shapes=[
            pltpu.VMEM((8, 512, 1024), jnp.bfloat16),
            pltpu.VMEM((16, 512, 512), jnp.bfloat16),
            pltpu.VMEM((16, 256, 2048), jnp.bfloat16),
            pltpu.VMEM((8, 512, 512), jnp.bfloat16),
            pltpu.VMEM((512, 512), jnp.float32),
            pltpu.VMEM((512, 2048), jnp.float32),
            dma((7, PARTS["A"])),
            dma((15, PARTS["G"])),
            dma((15, PARTS["F"])),
            dma((7, PARTS["L"])),
            dma((7, PARTS["A"])),
            dma((15, PARTS["G"])),
            dma((15, PARTS["F"])),
            dma((7, PARTS["L"])),
            dma((2, 8)),
            dma((2, 8)),
            dma((3,)),
            dma((PARTS["F"],)),
        ],
        compiler_params=pltpu.CompilerParams(
            collective_id=0, has_side_effects=True, vmem_limit_bytes=60 * 2**20
        ),
    )(grad_flat, out_factor_inv, in_factor_inv)


def solution(mesh):
    return jax.shard_map(
        per_device,
        mesh=mesh,
        in_specs=(P(("row", "col"), None), P("row", "col"), P(("row", "col"), None)),
        out_specs=P("row", "col"),
        check_vma=False,
    )
```

time: 376 us -> 184 us (0.49)
  waiting for transfers between devices: 288 us -> 0 us
  Pallas kernels: 0 us -> 179 us
  blocking collectives: 47.5 us -> 0 us
  matrix products: 25.9 us -> 0 us
  between operations: 13.2 us -> 0.01 us
    all_gather x4 -> x0, waiting for transfers between devices: 288 us -> none  [the longest x1 92.4 us: per_device(): factor_rows = lax.all_gather(out_factor_inv, 'col', axis=1, tiled=True)]
    pallas_call x0 -> x1, Pallas kernels: none -> 179 us  [per_device(): pl.pallas_call(functools.partial(kernel, order), out_shape=jax.ShapeDtype...]
    all_to_all x2 -> x0, blocking collectives: 47.5 us -> none  [the longest x1 28.6 us: per_device(): lax.all_to_all(in_factor_inv, 'col', split_axis=1, concat_axis=0, tiled=T...]
    dot_general x2 -> x0, matrix products: 25.9 us -> none  [the longest x1 14.9 us: per_device(): result = jnp.dot(product_wide, gathered, preferred_element_type=jnp.float32)]
    unnamed x2 -> x1, local copies, waits for them, and re-layouts: 0.01 us -> 4.7 us
  transfers between devices with their start and end apart: 4 -> 0, of which waited for: 4 -> 0; matrix products, arithmetic and copies ran while one was open for 0% -> 0% of each run, Pallas kernels for 0% -> 0%
where the time goes in v1:
time: 184 us
  Pallas kernels  179 us (97%)
  local copies, waits for them, and re-layouts  4.7 us (3%)
    pallas_call x1, Pallas kernels, per_device(): pl.pallas_call(functools.partial(kernel, order), out_shape=jax.ShapeDtype...  179 us
    unnamed x1, local copies, waits for them, and re-layouts  4.7 us

profile of v1, /device:TPU:1, one launch (start us, length us, event | category | flops | bytes accessed | tf_op | source)
XLA Modules:
  0.0 183.6 jit_solution(793379763556360210)
XLA Ops:
  0.0 178.9 %shard_map.37 = f32[512,2048]{1,0:T(8,128)} custom-call(bf16[64,4096]{1,0:T(8,128)(2,1)} %grad.1, bf16[512,1024]{1,0:T(8,128)(2,1)} %outer.1, bf16[32,16384]{1,0:T(8,128)(2,1)} %inner.1), custom_call_target="tpu_custom_call" | custom-call | tf_op jit(solution)/shard_map/pallas_call | solution.py:292
  178.9 4.7 %copy.5 = f32[512,2048]{1,0:T(8,128)} copy(f32[512,2048]{1,0:T(8,128)} %shard_map.37) | data formatting | bytes 8388608

commit v2 on v1

--- a/solution.py
+++ b/solution.py
@@ -11,62 +11,88 @@
 
 PARTS = {"A": 2, "L": 2, "G": 2, "F": 4}
 UNITS = {"A": 1.0, "L": 0.5, "G": 0.5, "F": 0.5}
-RELIEF = {"A": True, "L": True, "G": False, "F": False}
-OWN = -1
+RELIEF = {"A": False, "L": True, "G": False, "F": False}
+OWN, OWN_X, START = -1, -2, -3
+RELAYED = 4
+UNIT, LAG, FIFO = 12.0, 1.5, True
 
 
 def plan(array, slot, part):
     ahead, behind = ("+", "-") if part % 2 == 0 else ("-", "+")
     sends = {
-        OWN: [("x", 0), (ahead, 1), (behind, 2)],
+        OWN: [(ahead, 1), (behind, 2)],
+        OWN_X: [("x", 0)],
         0: [(ahead, 3)] + ([] if RELIEF[array] else [(behind, 4)]),
         1: [(ahead, 5)],
         2: [("x", 4)] if RELIEF[array] else [],
         4: [(behind, 6)],
     }.get(slot, [])
-    if array in "GF" and slot < 7:
+    if array in "GF" and OWN <= slot < 7:
         sends = sends + [("core", 8 + slot)]
     return sends
 
 
 def relative(slot, part):
     sibling, slot = (1, slot - 8) if slot >= 7 else (0, slot)
-    step, other = {OWN: (0, 0), 0: (0, 1), 1: (3, 0), 2: (1, 0), 3: (3, 1), 4: (1, 1), 5: (2, 0), 6: (2, 1)}[slot]
+    step, other = {OWN: (0, 0), OWN_X: (0, 0), 0: (0, 1), 1: (3, 0), 2: (1, 0), 3: (3, 1), 4: (1, 1), 5: (2, 0), 6: (2, 1)}[slot]
     return (step if part % 2 == 0 else (4 - step) % 4), other, sibling
 
 
 def schedule():
-    free, pending, order = {}, [], []
-    unit = 11.3
-
-    def send(now, array, slot, part):
+    now, active, timers, order, seen = 0.0, [], [], [], {}
+    swaps, starts, relayed = {("G", 0): 3, ("F", 0): 3}, {}, 0
+
+    def send(array, slot, part):
         for link, there in plan(array, slot, part):
             key = link if link in ("x", "core") else link + ("z" if array in "AL" else "y")
-            took = UNITS[array] * (unit if link != "core" else 1.8)
-            start = max(now, free.get(key, 0.0))
-            free[key] = start + took
-            pending.append((start + took + 1.0, array, there, part))
+            active.append([UNITS[array] * (UNIT if link != "core" else 1.8), key, (array, there, part)])
 
     for key in ("x", "+z", "-z"):
-        free[key] = 17.0
-    pending += [(1.0, "A", OWN, p) for p in range(PARTS["A"])]
-    pending += [(8.0, "G", OWN, p) for p in range(PARTS["G"])]
-    pending += [(24.0, "F", OWN, p) for p in range(PARTS["F"])]
-    seen = {}
-    while pending:
-        pending.sort()
-        event = pending.pop(0)
-        now, array, slot, part = event
-        order.append(event)
-        send(now, array, slot, part)
-        seen.setdefault((array, part), []).append(now)
-        if array == "G" and sum(len(seen.get(("G", p), [])) for p in range(PARTS["G"])) == 16 * PARTS["G"]:
-            seen["G"] = now
-        if array in "AG" and "G" in seen:
-            for p in range(PARTS["A"]):
-                if len(seen.get(("A", p), [])) == 8 and ("L", p) not in seen:
-                    seen[("L", p)] = []
-                    pending.append((now + 1.5, "L", OWN, p))
+        active.append([0.5 * UNIT, key, ("swap", "G", 0)])
+    timers += [(0.5, ("A", OWN, 0))]
+    while active or timers:
+        on = {}
+        for entry in active:
+            on.setdefault(entry[1], []).append(entry)
+        if FIFO:
+            on = {key: entries[:1] for key, entries in on.items()}
+        ends = [entry[0] * len(entries) for entries in on.values() for entry in entries]
+        step = min(ends + [max(0.0, t - now) for t, _ in timers])
+        now += step
+        for entries in on.values():
+            for entry in entries:
+                entry[0] -= step / len(entries)
+                if entry[0] < 1e-6:
+                    active.remove(entry)
+                    timers.append((now + LAG, entry[2]))
+        if "F" in starts and relayed >= RELAYED:
+            timers += [(now, event) for event in starts.pop("F")]
+        due = sorted(t for t in timers if t[0] <= now + 1e-6)
+        for timer in due:
+            timers.remove(timer)
+            array, slot, part = timer[1]
+            if array == "swap":
+                swaps[(slot, part)] -= 1
+                if swaps[(slot, part)] == 0:
+                    starts[slot] = [(slot, k, p) for k in (OWN_X, OWN) for p in range(PARTS[slot])]
+                    if slot == "G":
+                        timers += [(now, event) for event in starts.pop("G")]
+                        timers += [(now + 0.1, ('A', OWN_X, 0)), (now + 0.2, ('F', START, 0)), (now + 0.3, ('A', OWN, 1)), (now + 0.4, ('A', OWN_X, 1))]
+                continue
+            order.append((now, array, slot, part))
+            send(array, slot, part)
+            relayed += array == "G" and slot in (1, 4)
+            if slot == START:
+                for key in ("x", "+z", "-z"):
+                    active.append([1.0 * UNIT, key, ("swap", "F", 0)])
+            if slot < OWN:
+                continue
+            seen[(array, part)] = seen.get((array, part), 0) + 1
+            if all(seen.get(("G", p)) == 16 for p in range(PARTS["G"])):
+                for p in range(PARTS["A"]):
+                    if seen.get(("A", p)) == 8 and ("L", p, 0) not in seen:
+                        seen[("L", p, 0)] = 1
+                        timers += [(now + 1.5, ("L", OWN, p)), (now + 1.51, ("L", OWN_X, p))]
     return order
 
 
@@ -218,6 +244,7 @@
 
     counts = dict.fromkeys("AGFL", 0)
     counts.update({("F", p): 0 for p in range(PARTS["F"])})
+    begun = set()
     pending_left, ready_l, ready_f, out_copies = [], [], [], []
     blocks_l = {}
     done = [0] * PARTS["F"]
@@ -235,33 +262,33 @@
                     out_copies.append(out)
 
     for _, array, slot, part in order:
-        if slot == OWN:
-            if array == "A":
-                if part == 0:
-                    locals_[0].wait()
-                forward("A", OWN, part)
-                if part == PARTS["A"] - 1:
-                    start_swap(1)
-                    l_sum[...] = jnp.zeros_like(l_sum)
-
-                    @pl.loop(0, 8)
-                    def _(k):
-                        rows = pl.ds(pl.multiple_of(k * 64, 64), 64)
-                        c_sum[rows, :] = jnp.zeros((64, 2048), jnp.float32)
-            elif array == "L":
-                l_buf[col, pl.ds(part * 256, 256), :] = l_sum[pl.ds(part * 256, 256), :].astype(jnp.bfloat16)
-                forward("L", OWN, part)
-            else:
-                which = "GF".index(array)
-                if part == 0:
-                    locals_[1 + which].wait()
-                    for k in range(1, 8):
-                        swap_wait(which, k)
-                forward(array, OWN, part)
-        else:
+        if slot == START:
+            start_swap(1)
+            l_sum[...] = jnp.zeros_like(l_sum)
+
+            @pl.loop(0, 8)
+            def _(k):
+                rows = pl.ds(pl.multiple_of(k * 64, 64), 64)
+                c_sum[rows, :] = jnp.zeros((64, 2048), jnp.float32)
+
+            continue
+        if array in "GF" and array not in begun:
+            begun.add(array)
+            which = "GF".index(array)
+            locals_[1 + which].wait()
+            for k in range(1, 8):
+                swap_wait(which, k)
+        if array == "A" and array not in begun:
+            begun.add(array)
+            locals_[0].wait()
+        if array == "L" and slot == OWN:
+            l_buf[col, pl.ds(part * 256, 256), :] = l_sum[pl.ds(part * 256, 256), :].astype(jnp.bfloat16)
+        if slot >= 0:
             wait_recv(array, slot, part)
-            if slot < 7:
-                forward(array, slot, part)
+        if slot < 7:
+            forward(array, slot, part)
+        if slot < OWN:
+            continue
         counts[array] += 1
         if array == "A":
             pending_left.append((block_id("A", slot, part), part))

time: 184 us -> 145 us (0.79)
  Pallas kernels: 179 us -> 140 us
    pallas_call x1, Pallas kernels: 179 us -> 140 us  [per_device(): pl.pallas_call(functools.partial(kernel, order), out_shape=jax.ShapeDtype...]
where the time goes in v2:
time: 145 us
  Pallas kernels  140 us (97%)
  local copies, waits for them, and re-layouts  4.7 us (3%)
    pallas_call x1, Pallas kernels, per_device(): pl.pallas_call(functools.partial(kernel, order), out_shape=jax.ShapeDtype...  140 us
    unnamed x1, local copies, waits for them, and re-layouts  4.7 us

profile of v2, /device:TPU:1, one launch (start us, length us, event | category | flops | bytes accessed | tf_op | source)
XLA Modules:
  0.0 144.8 jit_solution(10697758739739073477)
XLA Ops:
  0.0 140.1 %shard_map.37 = f32[512,2048]{1,0:T(8,128)} custom-call(bf16[64,4096]{1,0:T(8,128)(2,1)} %grad.1, bf16[512,1024]{1,0:T(8,128)(2,1)} %outer.1, bf16[32,16384]{1,0:T(8,128)(2,1)} %inner.1), custom_call_target="tpu_custom_call" | custom-call | tf_op jit(solution)/shard_map/pallas_call | solution.py:319
  140.1 4.7 %copy.5 = f32[512,2048]{1,0:T(8,128)} copy(f32[512,2048]{1,0:T(8,128)} %shard_map.37) | data formatting | bytes 8388608

commit v3 on v2

--- a/solution.py
+++ b/solution.py
@@ -14,7 +14,8 @@
 RELIEF = {"A": False, "L": True, "G": False, "F": False}
 OWN, OWN_X, START = -1, -2, -3
 RELAYED = 4
-UNIT, LAG, FIFO = 12.0, 1.5, True
+STEP = 2
+UNIT, LAG, FIFO = 12.0, 3.0, True
 
 
 def plan(array, slot, part):
@@ -22,9 +23,9 @@
     sends = {
         OWN: [(ahead, 1), (behind, 2)],
         OWN_X: [("x", 0)],
-        0: [(ahead, 3)] + ([] if RELIEF[array] else [(behind, 4)]),
+        0: [(ahead, 3)] + ([] if RELIEF[array] or (array == "A" and part == 0) else [(behind, 4)]),
         1: [(ahead, 5)],
-        2: [("x", 4)] if RELIEF[array] else [],
+        2: [("x", 4)] if RELIEF[array] or (array == "A" and part == 0) else [],
         4: [(behind, 6)],
     }.get(slot, [])
     if array in "GF" and OWN <= slot < 7:
@@ -244,7 +245,7 @@
 
     counts = dict.fromkeys("AGFL", 0)
     counts.update({("F", p): 0 for p in range(PARTS["F"])})
-    begun = set()
+    begun, pending_c = set(), []
     pending_left, ready_l, ready_f, out_copies = [], [], [], []
     blocks_l = {}
     done = [0] * PARTS["F"]
@@ -282,6 +283,8 @@
             begun.add(array)
             locals_[0].wait()
         if array == "L" and slot == OWN:
+            each([u for u in pending_left if u[1] == part], add_left)
+            pending_left[:] = [u for u in pending_left if u[1] != part]
             l_buf[col, pl.ds(part * 256, 256), :] = l_sum[pl.ds(part * 256, 256), :].astype(jnp.bfloat16)
         if slot >= 0:
             wait_recv(array, slot, part)
@@ -293,19 +296,25 @@
         if array == "A":
             pending_left.append((block_id("A", slot, part), part))
         if array in "AG" and counts["G"] == 16 * PARTS["G"]:
-            each(pending_left, add_left)
-            pending_left.clear()
+            pass
         if array == "L":
             place = relative(slot, part)
             blocks_l[place] = blocks_l.get(place, 0) + 1
             if blocks_l[place] == PARTS["L"]:
                 ready_l.append(block_id("L", slot, part))
-                multiply([(ready_l[-1], p) for p in ready_f])
+                pending_c += [(ready_l[-1], p) for p in ready_f]
         if array == "F":
             counts[("F", part)] += 1
             if counts[("F", part)] == 16:
                 ready_f.append(part)
-                multiply([(block, part) for block in ready_l])
+                pending_c += [(block, part) for block in ready_l]
+        if counts["G"] == 16 * PARTS["G"] and pending_left:
+            each(pending_left[:STEP], add_left)
+            del pending_left[:STEP]
+        elif pending_c:
+            multiply(pending_c[:STEP])
+            del pending_c[:STEP]
+    multiply(pending_c)
 
     for one in sent:
         one.wait_send()

time: 145 us -> 137 us (0.945)
  Pallas kernels: 140 us -> 133 us
    pallas_call x1, Pallas kernels: 140 us -> 133 us  [per_device(): pl.pallas_call(functools.partial(kernel, order), out_shape=jax.ShapeDtype...]
where the time goes in v3:
time: 137 us
  Pallas kernels  133 us (97%)
  local copies, waits for them, and re-layouts  4.7 us (3%)
    pallas_call x1, Pallas kernels, per_device(): pl.pallas_call(functools.partial(kernel, order), out_shape=jax.ShapeDtype...  133 us
    unnamed x1, local copies, waits for them, and re-layouts  4.7 us

profile of v3, /device:TPU:1, one launch (start us, length us, event | category | flops | bytes accessed | tf_op | source)
XLA Modules:
  0.0 137.2 jit_solution(18265553496804733676)
XLA Ops:
  0.0 132.5 %shard_map.37 = f32[512,2048]{1,0:T(8,128)} custom-call(bf16[64,4096]{1,0:T(8,128)(2,1)} %grad.1, bf16[512,1024]{1,0:T(8,128)(2,1)} %outer.1, bf16[32,16384]{1,0:T(8,128)(2,1)} %inner.1), custom_call_target="tpu_custom_call" | custom-call | tf_op jit(solution)/shard_map/pallas_call | solution.py:328
  132.5 4.7 %copy.5 = f32[512,2048]{1,0:T(8,128)} copy(f32[512,2048]{1,0:T(8,128)} %shard_map.37) | data formatting | bytes 8388608

commit v4 on v3

--- a/solution.py
+++ b/solution.py
@@ -23,9 +23,9 @@
     sends = {
         OWN: [(ahead, 1), (behind, 2)],
         OWN_X: [("x", 0)],
-        0: [(ahead, 3)] + ([] if RELIEF[array] or (array == "A" and part == 0) else [(behind, 4)]),
+        0: [(ahead, 3)] + ([] if RELIEF[array] or (array == "A" and part == 1) else [(behind, 4)]),
         1: [(ahead, 5)],
-        2: [("x", 4)] if RELIEF[array] or (array == "A" and part == 0) else [],
+        2: [("x", 4)] if RELIEF[array] or (array == "A" and part == 1) else [],
         4: [(behind, 6)],
     }.get(slot, [])
     if array in "GF" and OWN <= slot < 7:

time: 137 us -> 138 us (level); the launches traced: 137 us -> 137 us
  no operation moved by 1% of the time
where the time goes in v4:
time: 138 us; the launch traced here: 137 us
  Pallas kernels  132 us (96%)
  local copies, waits for them, and re-layouts  4.7 us (3%)
    pallas_call x1, Pallas kernels, per_device(): pl.pallas_call(functools.partial(kernel, order), out_shape=jax.ShapeDtype...  132 us
    unnamed x1, local copies, waits for them, and re-layouts  4.7 us

profile of v4, /device:TPU:1, one launch (start us, length us, event | category | flops | bytes accessed | tf_op | source)
XLA Modules:
  0.0 136.8 jit_solution(9487070819949950597)
XLA Ops:
  0.0 132.1 %shard_map.37 = f32[512,2048]{1,0:T(8,128)} custom-call(bf16[64,4096]{1,0:T(8,128)(2,1)} %grad.1, bf16[512,1024]{1,0:T(8,128)(2,1)} %outer.1, bf16[32,16384]{1,0:T(8,128)(2,1)} %inner.1), custom_call_target="tpu_custom_call" | custom-call | tf_op jit(solution)/shard_map/pallas_call | solution.py:328
  132.1 4.7 %copy.5 = f32[512,2048]{1,0:T(8,128)} copy(f32[512,2048]{1,0:T(8,128)} %shard_map.37) | data formatting | bytes 8388608
